TPU v7x, 512 devices: a whole 4x8x8 slice. The times are simulated.
512 devices in a mesh: dp: 256 (over z_hi, y, x, core), mp: 2 (over z_lo).
Axes of the slice: x: 4, y: 8, z: 8 (z_hi: 4, z_lo: 2; z = z_hi * 2 + z_lo), core: 2. Of those that a mesh axis runs over, the one named last changes fastest.
Arguments:
- visual_encoder_outputs: bfloat16 [65536, 1152], P('dp'), may hold values from -6 to 6
- visual_mapping_matrix: bfloat16 [1152, 1152], P(None, 'mp'), may hold values from -0.1875 to 0.1875
- sentence_vectors_raw: bfloat16 [65536, 1152], P('dp', 'mp'), may hold values from -0.1796875 to 0.1796875
- matched_sentence_rows: int32 [65536], P('dp'), may hold values from 0 to 65535, as said below
- sharpness_coefficient: float32 [1], replicated, may hold values from 5 to 15
- pairwise_offset: float32 [1], replicated, may hold values from -4 to -1
Outputs:
- loss: float32 [1], replicated
- proj_grad: bfloat16 [1152, 1152], P(None, 'mp')
- caption_gradient: bfloat16 [65536, 1152], P('dp', 'mp')
Inputs may be any that keep to these rules, and one draw needn't show every extreme that they name: `matched_sentence_rows`: the matching text row of an image row in block b lies in block (b - s) mod 256 for some s of 0 .. 2, blocks of 256 rows.
All inputs are finite; a program needn't handle non-finite values.
Results may differ from a plain program's by a relative error of at most 0.014.
Values may be sent and summed in bfloat16 or wider, within the bound.
A program may use at most 64 MiB of HBM per device.

v0:
```python
import jax
import jax.numpy as jnp
from jax import lax
from jax.sharding import PartitionSpec as P

STEPS = 2


epsilon = 1e-06


def passed_along(value, axis, steps):
    count = lax.axis_size(axis)
    pairs = [(source, (source + steps) % count) for source in range(count)]
    return lax.ppermute(value, axis, pairs)


def unit_rows(values):
    norms = jnp.sqrt(jnp.sum(values * values, axis=1, keepdims=True) + epsilon)
    return (values / norms, norms)


def local(
    visual_encoder_outputs,
    visual_mapping_matrix,
    sentence_vectors_raw,
    matched_sentence_rows,
    sharpness_coefficient,
    pairwise_offset,
):
    row_count = visual_encoder_outputs.shape[0]
    proj_width = visual_mapping_matrix.shape[1]
    text_width = sentence_vectors_raw.shape[1]
    member = lax.axis_index("mp")
    anchor = lax.axis_index("dp")
    blocks = lax.axis_size("dp")
    similarity_multiplier = sharpness_coefficient[0]
    offset_b = pairwise_offset[0]
    text_full = lax.all_gather(sentence_vectors_raw, "mp", axis=1, tiled=True)
    raw_half = jnp.dot(
        visual_encoder_outputs, visual_mapping_matrix, preferred_element_type=jnp.float32
    )
    image_raw = lax.all_gather(raw_half, "mp", axis=1, tiled=True)
    image_unit, image_norm = unit_rows(image_raw)
    image_low = image_unit.astype(jnp.bfloat16)
    text_unit, text_norm = unit_rows(text_full.astype(jnp.float32))
    text_low = text_unit.astype(jnp.bfloat16)
    columns = jnp.arange(row_count, dtype=jnp.int32)
    my_low, my_unit, my_norm, my_pos = (image_low, image_unit, image_norm, matched_sentence_rows)
    text_block = text_low
    image_direction = jnp.zeros(my_unit.shape, jnp.float32)
    total = jnp.zeros((), jnp.float32)
    carried = jnp.zeros(text_unit.shape, jnp.float32)
    for stride in range(STEPS + 1):
        if stride > 0:
            text_block = passed_along(text_block, "dp", 1)
            carried = passed_along(carried.astype(jnp.bfloat16), "dp", 1).astype(carried.dtype)
        owner = (anchor - stride) % blocks
        ids = owner * row_count + columns
        logits = (
            similarity_multiplier
            * lax.dot_general(
                my_low, text_block, (((1,), (1,)), ((), ())), preferred_element_type=jnp.float32
            )
            + offset_b
        )
        signs = jnp.where(my_pos[:, None] == ids[None, :], 1.0, -1.0).astype(jnp.float32)
        loss_part = jnp.sum(jax.nn.softplus(-signs * logits))
        weight = (-signs * jax.nn.sigmoid(-signs * logits) * similarity_multiplier).astype(
            jnp.bfloat16
        )
        image_part = jnp.dot(weight, text_block, preferred_element_type=jnp.float32)
        text_part = lax.dot_general(
            weight, my_low, (((0,), (0,)), ((), ())), preferred_element_type=jnp.float32
        )
        loss_part, image_part, text_part = (loss_part, image_part, text_part)
        total = total + loss_part
        image_direction = image_direction + image_part
        carried = text_part if stride == 0 else carried + text_part
    text_direction = passed_along(carried.astype(jnp.bfloat16), "dp", -STEPS).astype(carried.dtype)
    image_back = (
        (image_direction - my_unit * jnp.sum(my_unit * image_direction, axis=1, keepdims=True))
        / my_norm
    ).astype(jnp.bfloat16)
    back_half = lax.dynamic_slice_in_dim(image_back, member * proj_width, proj_width, 1)
    text_back = (
        text_direction - text_unit * jnp.sum(text_unit * text_direction, axis=1, keepdims=True)
    ) / text_norm
    caption_gradient = lax.dynamic_slice_in_dim(
        text_back, member * text_width, text_width, 1
    ).astype(jnp.bfloat16)
    grad_part = lax.dot_general(
        visual_encoder_outputs,
        back_half,
        (((0,), (0,)), ((), ())),
        preferred_element_type=jnp.float32,
    )
    gradient_total, loss_sum = lax.psum((grad_part, total), "dp")
    loss = (loss_sum / (row_count * blocks)).reshape(1)
    return (loss, gradient_total.astype(jnp.bfloat16), caption_gradient)


def solution(mesh):
    placed = (P("dp", None), P(None, "mp"), P("dp", "mp"), P("dp"), P(), P())
    return jax.shard_map(
        local,
        mesh=mesh,
        in_specs=placed,
        out_specs=(P(), P(None, "mp"), P("dp", "mp")),
        check_vma=False,
    )
```

profile of v0, /device:TPU:1, one launch (start us, length us, event | category | flops | bytes accessed | tf_op | source)
XLA Modules:
  0.0 1525.2 jit_solution(647523138288012284)
XLA Ops:
  7.2 1.3 copy-done
  8.5 2.5 fusion.23
  11.0 7.7 all_gather.7
  19.2 1.1 fusion.21
  20.3 6.8 collective-permute-start
  28.5 19.0 %all-gather.2.cloned.1.call-done = f32[256,1152]{0,1:T(8,128)} async-done(((f32[256,576]{0,1:T(8,128)}), f32[256,1152]{0,1:T(8,128)}) %all-gather.2.cloned.1.call-update) | async-done | bytes 1179664 | tf_op jit(solution)/shard_map/all_gather | solution.py:43
  47.4 1.5 multiply_reduce_fusion.2
  49.2 0.5 copy-done.6
  49.8 2.3 fusion.14
  52.0 1.3 convolution_convert_fusion
  53.3 3.6 collective-permute-start.2
  57.0 1.9 collective-permute-start.1
  58.9 2.4 fusion.15
  61.3 1.6 fusion.18
  62.9 1.2 collective-permute-done.2
  64.1 1.5 add_convert_fusion.1
  65.7 4.4 collective-permute-start.3
  70.1 0.4 collective-permute-done.1
  70.4 1.1 fusion.16
  71.6 0.5 fusion.20
  72.0 1.5 convolution_add_fusion.1
  73.6 9.9 collective-permute-done.3
  83.4 0.9 add_convert_fusion
  84.4 18.4 %collective-permute-start.4 = (bf16[256,1152]{1,0:T(8,128)(2,1)}, bf16[256,1152]{1,0:T(8,128)(2,1)}, u32[]{:S(2)}, u32[]{:S(2)}) collective-permute-start(bf16[256,1152]{1,0:T(8,128)(2,1)} %add_convert_fusion), channel_id=1, source_target_pairs={{0,508},{2,510},{4,0},{6,2},{8,4},{10,6},{12,8},{14,10},{16,12},{1... | collective-permute-start | bytes 1769480 | tf_op jit(solution)/shard_map/ppermute | solution.py:15
  102.8 0.5 multiply_reduce_fusion.1
  103.3 0.5 copy-done.2
  103.9 2.1 convolution_bitcast_fusion
  107.8 1404.8 %all-reduce.2 = (f32[]{:T(128)}, bf16[1152,576]{0,1:T(8,128)(2,1)}) all-reduce(f32[]{:T(128)S(6)} %add.136, f32[1152,576]{0,1:T(8,128)} %convolution_bitcast_fusion), channel_id=1, replica_groups=mesh['dp'=256,'mp'=2] {'dp'}, use_global_device_ids=true, to_apply=%region_5.6 | all-reduce | flops 663553 | bytes 3981320 | tf_op jit(solution)/shard_map/psum | solution.py:98
  1513.3 1.4 multiply_reduce_fusion
  1514.7 1.1 convert_element_type.58
  1515.8 0.5 fusion.8
  1516.3 0.9 copy.18
  (23 shorter events, 0.8 us)
Async XLA Ops:
  7.2 1.3 copy-start
  7.2 3.8 copy-start.5
  7.2 40.3 %all-gather.2.cloned.1.call-start = ((), (), s32[]{:S(2)}) async-start(), calls=%async_computation | async-start | bytes 1769472 | tf_op jit(solution)/shard_map/all_gather | solution.py:43
  20.3 36.7 %collective-permute-start = (bf16[256,1152]{1,0:T(8,128)(2,1)}, bf16[256,1152]{1,0:T(8,128)(2,1)}, u32[]{:S(2)}, u32[]{:S(2)}) collective-permute-start(bf16[256,1152]{1,0:T(8,128)(2,1)} %fusion.21), channel_id=1, source_target_pairs={{0,2},{2,4},{4,6},{6,8},{8,10},{10,12},{12,14},{14,16},{16,18},{18... | collective-permute-start | bytes 1769480 | tf_op jit(solution)/shard_map/ppermute | solution.py:15
  47.4 1.6 copy-start.1
  49.1 0.7 copy-start.6
  49.2 4.1 copy-start.3
  53.3 10.8 collective-permute-start.2
  57.0 13.4 collective-permute-start.1
  61.3 2.8 copy-start.4
  65.7 17.8 %collective-permute-start.3 = (bf16[256,1152]{1,0:T(8,128)(2,1)S(1)}, bf16[256,1152]{1,0:T(8,128)(2,1)S(1)}, u32[]{:S(2)}, u32[]{:S(2)}) collective-permute-start(bf16[256,1152]{1,0:T(8,128)(2,1)S(1)} %add_convert_fusion.1), channel_id=1, source_target_pairs={{0,2},{2,4},{4,6},{6,8},{8,10},{10,12},{12,14},{14,16},{16,18},{18... | collective-permute-start | bytes 1769480 | tf_op jit(solution)/shard_map/ppermute | solution.py:15
  84.4 1428.9 %collective-permute-start.4 = (bf16[256,1152]{1,0:T(8,128)(2,1)}, bf16[256,1152]{1,0:T(8,128)(2,1)}, u32[]{:S(2)}, u32[]{:S(2)}) collective-permute-start(bf16[256,1152]{1,0:T(8,128)(2,1)} %add_convert_fusion), channel_id=1, source_target_pairs={{0,508},{2,510},{4,0},{6,2},{8,4},{10,6},{12,8},{14,10},{16,12},{1... | collective-permute-start | bytes 1769480 | tf_op jit(solution)/shard_map/ppermute | solution.py:15
  102.8 1.1 copy-start.2
Sparse Core Ops, SparseCore 0:
  11.1 36.2 all-gather.1
where the time goes:
time: 1530 us
  blocking collectives  1410 us (92%)
  starting transfers between devices  35.3 us (2%)
  waiting for transfers between devices  30.4 us (2%)
  between operations  19.2 us (1%)
  matrix products  17.2 us (1%)
    psum x1, blocking collectives, local(): gradient_total, loss_sum = lax.psum((grad_part, total), 'dp')  1400 us
    ppermute x5, starting transfers between devices, passed_along(): return lax.ppermute(value, axis, pairs)  35.2 us
  transfers between devices with their start and end apart: 6, of which 4 were waited for; matrix products, arithmetic and copies ran while one was open for 1% of the time, Pallas kernels for 0%

commit v1 on v0

v1 whole, which is shorter than its diff:
```python
import functools

import jax
import jax.numpy as jnp
from jax import lax
from jax.experimental import pallas as pl
from jax.experimental.pallas import tpu as pltpu
from jax.sharding import PartitionSpec as P

STEPS = 2
NX, NY, NZ = 4, 8, 4
BLOCKS = NX * NY * NZ * 2
EPSILON = 1e-06
ROW_TILE = 16
LANES = 128
MESH = pl.DeviceIdType.MESH
F32, BF16 = jnp.float32, jnp.bfloat16


def dot(a, b, over_a, over_b):
    return lax.dot_general(a, b, (((over_a,), (over_b,)), ((), ())), preferred_element_type=F32)


def up(value, step):
    return -(-value // step)


def sizes(width, depth):
    full = (width // 2) * (depth // LANES)
    of_x = up(full // ROW_TILE, NX) * ROW_TILE
    of_y = up(of_x // ROW_TILE, NY) * ROW_TILE
    of_z = up(of_y // ROW_TILE, NZ) * ROW_TILE
    return full, of_x, of_y, of_z


class Copies:
    def __init__(self, send_sem, recv_sem):
        self.send_sem, self.recv_sem, self.made = send_sem, recv_sem, []

    def start(self, source, target, device):
        i = len(self.made)
        copy = pltpu.make_async_remote_copy(
            src_ref=source,
            dst_ref=target,
            send_sem=self.send_sem.at[i],
            recv_sem=self.recv_sem.at[i],
            device_id=device,
            device_id_type=MESH,
        )
        copy.start()
        self.made.append(copy)
        return copy


def kernel(
    x_hbm,
    w_hbm,
    t_hbm,
    matched_ref,
    scale_ref,
    offset_ref,
    loss_ref,
    flat_ref,
    cap_ref,
    x_all,
    w_ref,
    text_raw,
    text_low,
    image_unit,
    image_low,
    sums_out,
    sums_in,
    text_sums,
    cos_out,
    cos_in,
    weight,
    back,
    back_all,
    g_x,
    g_y,
    g_z,
    h_z,
    h_y,
    r_x,
    r_y,
    r_z,
    loss_core,
    loss_x,
    loss_y,
    loss_z,
    text_part,
    text_in,
    tdot_out,
    tdot_in,
    load_sem,
    send_sem,
    recv_sem,
):
    width, rows = t_hbm.shape
    depth = x_hbm.shape[1]
    half = width // 2
    full, of_x, of_y, of_z = sizes(width, depth)
    dp, mp = lax.axis_index("dp"), lax.axis_index("mp")
    core = lax.rem(dp, 2)
    x = lax.rem(dp // 2, NX)
    y = lax.rem(dp // (2 * NX), NY)
    z = dp // (2 * NX * NY)
    other_mp = (dp, 1 - mp)
    other_core = (dp + 1 - 2 * core, mp)

    def along_dp(step):
        return (lax.rem(dp + step + BLOCKS, BLOCKS), mp)

    def along(count, at, stride):
        places = [lax.rem(at + k, count) for k in range(1, count)]
        return [(place, (dp + (place - at) * stride, mp)) for place in places]

    def source_of(count, at, k):
        return lax.rem(at - k + count, count)

    on_x, on_y, on_z = along(NX, x, 2), along(NY, y, 2 * NX), along(NZ, z, 2 * NX * NY)

    loads = [
        pltpu.make_async_copy(t_hbm, text_raw.at[0], load_sem.at[0]),
        pltpu.make_async_copy(w_hbm, w_ref, load_sem.at[1]),
        pltpu.make_async_copy(x_hbm, x_all.at[core], load_sem.at[2]),
    ]
    for load in loads:
        load.start()

    barrier = pltpu.get_barrier_semaphore()
    greeted = [other_mp, other_core] + [along_dp(s) for s in (-2, -1, 1, 2)]
    greeted += [device for _, device in on_x + on_y + on_z]
    for device in greeted:
        pl.semaphore_signal(barrier, inc=1, device_id=device, device_id_type=MESH)
    pl.semaphore_wait(barrier, len(greeted))

    copies = Copies(send_sem, recv_sem)
    send = copies.start
    text_there = [send(t_hbm, text_raw.at[s], along_dp(s)) for s in (1, 2)]

    for load in loads:
        load.wait()
    x_there = send(x_all.at[core], x_all.at[core], other_core)
    image_raw = dot(w_ref[...], x_all[core], 1, 1)
    own_text = text_raw[0].astype(F32)
    sums_out[0:1, :] = jnp.sum(image_raw * image_raw, axis=0, keepdims=True)
    sums_out[1:2, :] = jnp.sum(own_text * own_text, axis=0, keepdims=True)
    sums_there = send(sums_out, sums_in, other_mp)
    sums_there.wait_recv()
    sums = sums_out[...] + sums_in[...]
    image_scale = lax.rsqrt(sums[0:1, :] + EPSILON)
    text_scale = lax.rsqrt(sums[1:2, :] + EPSILON)
    text_sums[0] = sums
    text_sums_there = [send(text_sums.at[0], text_sums.at[s], along_dp(s)) for s in (1, 2)]
    unit = image_raw * image_scale
    image_unit[...] = unit
    image_low[...] = unit.astype(BF16)

    cos_there = []
    for s in range(STEPS + 1):
        if s > 0:
            text_there[s - 1].wait_recv()
            text_sums_there[s - 1].wait_recv()
            text_low[s] = (
                text_raw[s].astype(F32) * lax.rsqrt(text_sums[s, 1:2, :] + EPSILON)
            ).astype(BF16)
        else:
            text_low[0] = (own_text * text_scale).astype(BF16)
        cos_out[s] = dot(text_low[s], image_low[...], 0, 0).astype(BF16)
        cos_there.append(send(cos_out.at[s], cos_in.at[s], other_mp))

    sharpness, offset = scale_ref[0], offset_ref[0]
    loss_rows = jnp.zeros((1, rows), F32)
    along_unit = jnp.zeros((1, rows), F32)
    direction = jnp.zeros((width, rows), F32)
    for s in range(STEPS + 1):
        cos_there[s].wait_recv()
        cos = cos_out[s].astype(F32) + cos_in[s].astype(F32)
        ids = lax.rem(dp - s + BLOCKS, BLOCKS) * rows + lax.broadcasted_iota(jnp.int32, (rows, rows), 0)
        matched = ids == matched_ref[...]
        logit = sharpness * cos + offset
        against = jnp.where(matched, -logit, logit)
        small = jnp.exp(-jnp.abs(against))
        loss_rows += jnp.sum(jnp.maximum(against, 0.0) + jnp.log1p(small), axis=0, keepdims=True)
        sigmoid = jnp.where(against >= 0.0, 1.0, small) / (1.0 + small)
        low = (jnp.where(matched, -sigmoid, sigmoid) * sharpness).astype(BF16)
        weight[s] = low
        along_unit += jnp.sum(low.astype(F32) * cos, axis=0, keepdims=True)
        direction += dot(text_low[s], low, 1, 0)

    image_back = ((direction - image_unit[...] * along_unit) * image_scale).astype(BF16)
    back[0] = image_back[:half]
    back[1] = image_back[half:]
    back_there = send(back.at[1 - core], back_all.at[core], other_core)
    back_all[core] = back[core]
    lanes = loss_rows[:, : rows // 2] + loss_rows[:, rows // 2 :]
    if rows // 2 < LANES:
        lanes = jnp.concatenate([lanes, jnp.zeros((1, LANES - rows // 2), F32)], axis=1)
    loss_core[core] = jnp.broadcast_to(lanes, (8, LANES))
    loss_core_there = send(loss_core.at[core], loss_core.at[core], other_core)

    x_there.wait_recv()
    back_there.wait_recv()
    mine, others = back_all[core], back_all[1 - core]
    x_mine, x_others = x_all[core], x_all[1 - core]
    for k in range(depth // LANES):
        cols = slice(k * LANES, (k + 1) * LANES)
        part = dot(mine, x_mine[:, cols], 1, 0) + dot(others, x_others[:, cols], 1, 0)
        g_x[k * half : (k + 1) * half, :] = part.astype(BF16)
    if NX * of_x > full:
        g_x[full:, :] = jnp.zeros((NX * of_x - full, LANES), BF16)

    def rows_of(ref, place, count):
        return ref.at[pl.ds(pl.multiple_of(place * count, ROW_TILE), count)]

    def scatter(places, full_ref, count, landing, own_place, loss_landing, loss_now):
        there = [
            send(rows_of(full_ref, place, count), landing.at[k], device)
            for k, (place, device) in enumerate(places)
        ]
        loss_landing[own_place] = loss_now
        loss_sent = [
            send(loss_landing.at[own_place], loss_landing.at[own_place], device)
            for _, device in places
        ]
        return there, loss_sent

    def gather_sum(there, full_ref, count, landing, own_place):
        total = rows_of(full_ref, own_place, count)[...].astype(F32)
        for k, copy in enumerate(there):
            copy.wait_recv()
            total += landing[k].astype(F32)
        return total

    def loss_sum(loss_sent, loss_landing, count):
        for copy in loss_sent:
            copy.wait_recv()
        total = loss_landing[0]
        for k in range(1, count):
            total += loss_landing[k]
        return total

    loss_core_there.wait_recv()
    there, loss_sent = scatter(on_x, g_x, of_x, r_x, x, loss_x, loss_core[0] + loss_core[1])
    own_part = dot(image_low[...], weight[0], 1, 1)
    for s in (1, 2):
        text_part[s - 1] = dot(image_low[...], weight[s], 1, 1).astype(BF16)
    total = gather_sum(there, g_x, of_x, r_x, x)
    g_y[:of_x, :] = total.astype(BF16)
    if NY * of_y > of_x:
        g_y[of_x:, :] = jnp.zeros((NY * of_y - of_x, LANES), BF16)
    loss_now = loss_sum(loss_sent, loss_x, NX)

    there, loss_sent = scatter(on_y, g_y, of_y, r_y, y, loss_y, loss_now)
    parts_there = [send(text_part.at[s - 1], text_in.at[s - 1], along_dp(-s)) for s in (1, 2)]
    total = gather_sum(there, g_y, of_y, r_y, y)
    g_z[:of_y, :] = total.astype(BF16)
    if NZ * of_z > of_y:
        g_z[of_y:, :] = jnp.zeros((NZ * of_z - of_y, LANES), BF16)
    loss_now = loss_sum(loss_sent, loss_y, NY)

    there, loss_sent = scatter(on_z, g_z, of_z, r_z, z, loss_z, loss_now)
    total = gather_sum(there, g_z, of_z, r_z, z)
    own_z = rows_of(h_z, z, of_z)
    own_z[...] = total.astype(BF16)

    there = [send(own_z, own_z, device) for _, device in on_z]
    loss_now = loss_sum(loss_sent, loss_z, NZ)
    loss_ref[0] = jnp.sum(loss_now[0:1, :]) / (rows * BLOCKS)
    for copy in there:
        copy.wait_recv()
    own_y = rows_of(h_y, y, of_y)
    own_y[...] = h_z[:of_y, :]
    there = [send(own_y, own_y, device) for _, device in on_y]

    for copy in parts_there:
        copy.wait_recv()
    text_dir = own_part + text_in[0].astype(F32) + text_in[1].astype(F32)
    text_unit = text_raw[0].astype(F32) * text_scale
    tdot = jnp.sum(text_unit * text_dir, axis=0, keepdims=True)
    tdot_out[...] = jnp.broadcast_to(tdot, tdot_out.shape)
    tdot_there = send(tdot_out, tdot_in, other_mp)

    for copy in there:
        copy.wait_recv()

    def chunk(place):
        return flat_ref.at[core, pl.ds(pl.multiple_of(place * of_x, ROW_TILE), of_x)]

    chunk(x)[...] = h_y[:of_x, :]
    there = [send(chunk(x), chunk(x), device) for _, device in on_x]
    relayed = [send(chunk(x), chunk(x), other_core)]
    tdot_there.wait_recv()
    tdot = tdot_out[0:1, :] + tdot_in[0:1, :]
    cap_ref[...] = ((text_dir - text_unit * tdot) * text_scale).astype(BF16)
    for k, copy in enumerate(there):
        copy.wait_recv()
        place = source_of(NX, x, k + 1)
        relayed.append(send(chunk(place), chunk(place), other_core))
    for copy in relayed:
        copy.wait_recv()
    for copy in copies.made:
        copy.wait_send()


def local(x_rows, w_half, t_half, matched, sharpness, offset):
    rows, depth = x_rows.shape
    width = w_half.shape[1]
    half = width // 2
    full, of_x, of_y, of_z = sizes(width, depth)
    n_copies = 2 + 1 + 1 + 2 + 3 + 2 + 3 * (NX + NY + NZ - 3) + 2 + 1 + 1 + (NX - 1)
    vmem, whole = pl.BlockSpec(memory_space=pltpu.VMEM), pl.BlockSpec(memory_space=pl.ANY)
    smem = pl.BlockSpec(memory_space=pltpu.SMEM)
    flat_shape = (2, NX * of_x, LANES)
    call = pl.pallas_call(
        kernel,
        out_shape=(
            jax.ShapeDtypeStruct((1,), F32),
            jax.ShapeDtypeStruct(flat_shape, BF16),
            jax.ShapeDtypeStruct((width, rows), BF16),
        ),
        in_specs=[whole, whole, whole, vmem, smem, smem],
        out_specs=(smem, vmem, vmem),
        scratch_shapes=[
            pltpu.VMEM((2, rows, depth), BF16),
            pltpu.VMEM((width, depth), BF16),
            pltpu.VMEM((3, width, rows), BF16),
            pltpu.VMEM((3, width, rows), BF16),
            pltpu.VMEM((width, rows), F32),
            pltpu.VMEM((width, rows), BF16),
            pltpu.VMEM((8, rows), F32),
            pltpu.VMEM((8, rows), F32),
            pltpu.VMEM((3, 8, rows), F32),
            pltpu.VMEM((3, rows, rows), BF16),
            pltpu.VMEM((3, rows, rows), BF16),
            pltpu.VMEM((3, rows, rows), BF16),
            pltpu.VMEM((2, half, rows), BF16),
            pltpu.VMEM((2, half, rows), BF16),
            pltpu.VMEM((NX * of_x, LANES), BF16),
            pltpu.VMEM((NY * of_y, LANES), BF16),
            pltpu.VMEM((NZ * of_z, LANES), BF16),
            pltpu.VMEM((NZ * of_z, LANES), BF16),
            pltpu.VMEM((NY * of_y, LANES), BF16),
            pltpu.VMEM((NX - 1, of_x, LANES), BF16),
            pltpu.VMEM((NY - 1, of_y, LANES), BF16),
            pltpu.VMEM((NZ - 1, of_z, LANES), BF16),
            pltpu.VMEM((2, 8, LANES), F32),
            pltpu.VMEM((NX, 8, LANES), F32),
            pltpu.VMEM((NY, 8, LANES), F32),
            pltpu.VMEM((NZ, 8, LANES), F32),
            pltpu.VMEM((2, width, rows), BF16),
            pltpu.VMEM((2, width, rows), BF16),
            pltpu.VMEM((8, rows), F32),
            pltpu.VMEM((8, rows), F32),
            pltpu.SemaphoreType.DMA((3,)),
            pltpu.SemaphoreType.DMA((n_copies,)),
            pltpu.SemaphoreType.DMA((n_copies,)),
        ],
        compiler_params=pltpu.CompilerParams(
            collective_id=0, has_side_effects=True, vmem_limit_bytes=40 * 1024 * 1024
        ),
    )
    loss, flat, cap = call(
        x_rows, w_half.T, t_half.T, matched.reshape(1, rows), sharpness, offset
    )
    tiles = flat[:, :full].reshape(2, depth // LANES, half, LANES)
    grad = tiles.transpose(0, 2, 1, 3).reshape(width, depth)
    return (loss, grad.T, cap.T)


def solution(mesh):
    placed = (P("dp", None), P(None, "mp"), P("dp", "mp"), P("dp"), P(), P())
    return jax.shard_map(
        local,
        mesh=mesh,
        in_specs=placed,
        out_specs=(P(), P(None, "mp"), P("dp", "mp")),
        check_vma=False,
    )
```

time: 1530 us -> 111 us (0.07)
  the two profiles are of different devices: /device:TPU:1 before, /device:TPU:21 now
where the time goes in v1:
time: 111 us
  Pallas kernels  97.4 us (88%)
  local copies, waits for them, and re-layouts  9.74 us (9%)
  between operations  3.72 us (3%)
    pallas_call x1, Pallas kernels, local(): call(x_rows, w_half.T, t_half.T, matched.reshape(1, rows), sharpness, off...  97.4 us
    unnamed x10, local copies, waits for them, and re-layouts  6.5 us

profile of v1, /device:TPU:21, one launch (start us, length us, event | category | flops | bytes accessed | tf_op | source)
XLA Modules:
  0.0 110.8 jit_solution(16967757493327895550)
XLA Ops:
  1.9 0.0 copy-start
  1.9 1.3 %copy-done = bf16[1152,576]{0,1:T(8,128)(2,1)S(1)} copy-done((bf16[1152,576]{0,1:T(8,128)(2,1)S(1)}, bf16[1152,576]{0,1:T(8,128)(2,1)}, u32[]{:S(2)}) %copy-start) | copy-done | bytes 1327128
  3.2 0.0 copy-start.1
  3.2 1.1 copy-done.1
  4.3 0.0 copy-start.2
  4.3 1.0 copy-done.2
  5.3 0.0 copy-start.3
  5.3 0.7 copy-done.3
  6.0 97.4 %shard_map.85 = (f32[1]{0:T(128)}, bf16[2,2624,128]{2,1,0:T(8,128)(2,1)S(1)}, bf16[576,256]{1,0:T(8,128)(2,1)S(1)}) custom-call(bf16[256,1152]{1,0:T(8,128)(2,1)S(1)} %copy-done.1, bf16[576,1152]{1,0:T(8,128)(2,1)S(1)} %bitcast.9, bf16[576,256]{1,0:T(8,128)(2,1)S(1)} %bitcast.10, s32[1,256]{1,0:T(1,128)S(1)} %bitcast.12, f32[1]{0:T(128)S(6)} %copy.14.scale_ref, ...), custom_call_target="tpu_custom_call" | custom-call | tf_op jit(solution)/shard_map/pallas_call | solution.py:364
  103.3 0.1 slice.3
  103.4 1.9 %copy.10 = bf16[2,9,288,128]{2,0,3,1:T(2,128)(2,1)S(1)} copy(bf16[2,9,288,128]{3,2,1,0:T(8,128)(2,1)S(1)} %bitcast.15) | data formatting | bytes 2654208 | tf_op jit(solution)/shard_map/reshape | solution.py:367
  105.3 1.2 %reshape.17 = bf16[576,1152]{0,1:T(8,128)(2,1)S(1)} reshape(bf16[2,288,9,128]{1,0,3,2:T(2,128)(2,1)S(1)} %bitcast.13) | data formatting | bytes 2654208 | tf_op jit(solution)/shard_map/reshape | solution.py:368
  106.6 1.8 %copy.11 = bf16[1152,576]{0,1:T(8,128)(2,1)} copy(bf16[1152,576]{1,0:T(8,128)(2,1)S(1)} %bitcast.14) | data formatting | bytes 2654208
  109.0 0.7 copy.17
Async XLA Ops:
  1.9 1.3 %copy-start = (bf16[1152,576]{0,1:T(8,128)(2,1)S(1)}, bf16[1152,576]{0,1:T(8,128)(2,1)}, u32[]{:S(2)}) copy-start(bf16[1152,576]{0,1:T(8,128)(2,1)} %param.7) | copy-start | bytes 3981316
  3.2 1.1 copy-start.1
  4.3 1.0 copy-start.2
  5.3 0.7 copy-start.3

commit v2 on v1

v2 whole, which is shorter than its diff:
```python
import jax
import jax.numpy as jnp
from jax import lax
from jax.experimental import pallas as pl
from jax.experimental.pallas import tpu as pltpu
from jax.sharding import PartitionSpec as P

STEPS = 2
NX, NY, NZ = 4, 8, 4
BLOCKS = NX * NY * NZ * 2
EPSILON = 1e-06
ROW_TILE = 16
LANES = 128
N_COPIES = 128
MESH = pl.DeviceIdType.MESH
F32, BF16 = jnp.float32, jnp.bfloat16


def dot(a, b, over_a, over_b):
    return lax.dot_general(a, b, (((over_a,), (over_b,)), ((), ())), preferred_element_type=F32)


def groups_of(width, depth):
    half, tiles = width // 2, depth // LANES
    cut = tiles * 2 // 3
    groups = []
    for first, last, order in ((0, cut, "xyz"), (cut, tiles, "yxz")):
        counts = [{"x": NX, "y": NY, "z": NZ}[axis] for axis in order]
        held = [(last - first) * half]
        for count in counts:
            held.append(-(-held[-1] // (count * ROW_TILE)) * ROW_TILE)
        groups.append((first, last, order, counts, held))
    return groups


class Copies:
    def __init__(self, send_sem, recv_sem):
        self.send_sem, self.recv_sem, self.made = send_sem, recv_sem, []

    def start(self, source, target, device):
        i = len(self.made)
        copy = remote(source, target, self.send_sem.at[i], self.recv_sem.at[i], device)
        copy.start()
        self.made.append(copy)
        return copy


def remote(source, target, send_sem, recv_sem, device):
    return pltpu.make_async_remote_copy(
        src_ref=source,
        dst_ref=target,
        send_sem=send_sem,
        recv_sem=recv_sem,
        device_id=device,
        device_id_type=MESH,
    )


def rows_of(ref, place, count):
    return ref.at[pl.ds(pl.multiple_of(place * count, ROW_TILE), count)]


def kernel(
    x_hbm,
    w_hbm,
    t_hbm,
    matched_ref,
    scale_ref,
    offset_ref,
    loss_ref,
    grad_ref,
    cap_ref,
    x_all,
    w_ref,
    text_raw,
    text_low,
    image_unit,
    image_low,
    sums_out,
    sums_in,
    text_sums,
    cos_out,
    cos_in,
    weight,
    back,
    back_all,
    loss_core,
    loss_x,
    loss_y,
    loss_z,
    text_dir,
    text_part,
    presum_in,
    presum_out,
    text_in,
    tdot_out,
    tdot_in,
    *rest,
):
    *buffers, load_sem, text_send, text_recv, cos_send, cos_recv, part_send, part_recv, send_sem, recv_sem = rest
    width, rows = t_hbm.shape
    depth = x_hbm.shape[1]
    half, hr = width // 2, rows // 2
    dp, mp = lax.axis_index("dp"), lax.axis_index("mp")
    core = lax.rem(dp, 2)
    at = {"x": lax.rem(dp // 2, NX), "y": lax.rem(dp // (2 * NX), NY), "z": dp // (2 * NX * NY)}
    counts = {"x": NX, "y": NY, "z": NZ}
    strides = {"x": 2, "y": 2 * NX, "z": 2 * NX * NY}
    other_mp = (dp, 1 - mp)
    other_core = (dp + 1 - 2 * core, mp)

    def along_dp(step):
        return (lax.rem(dp + step + BLOCKS, BLOCKS), mp)

    def others(axis):
        places = [lax.rem(at[axis] + k, counts[axis]) for k in range(1, counts[axis])]
        return [(place, (dp + (place - at[axis]) * strides[axis], mp)) for place in places]

    def source_of(axis, k):
        return lax.rem(at[axis] - k + counts[axis], counts[axis])

    halves = [t_hbm.at[:, :hr], t_hbm.at[:, hr:]]
    loads = [
        pltpu.make_async_copy(halves[0], text_raw.at[0, 0], load_sem.at[0]),
        pltpu.make_async_copy(halves[1], text_raw.at[0, 1], load_sem.at[1]),
        pltpu.make_async_copy(w_hbm, w_ref, load_sem.at[2]),
        pltpu.make_async_copy(x_hbm, x_all.at[core], load_sem.at[3]),
    ]
    for load in loads:
        load.start()

    barrier = pltpu.get_barrier_semaphore()
    greeted = [other_mp, other_core] + [along_dp(s) for s in (-2, -1, 1, 2)]
    greeted += [device for axis in "xyz" for _, device in others(axis)]
    for device in greeted:
        pl.semaphore_signal(barrier, inc=1, device_id=device, device_id_type=MESH)
    pl.semaphore_wait(barrier, len(greeted))

    copies = Copies(send_sem, recv_sem)
    send = copies.start

    def text_copy(h, step, number):
        return remote(
            halves[h],
            text_raw.at[step, h],
            text_send.at[number],
            text_recv.at[step - 1, h],
            along_dp(step),
        )

    both = [text_copy(0, 1, 0), text_copy(1, 2, 1)]
    first_only = [text_copy(0, 2, 2), text_copy(1, 1, 3)]
    for copy in both:
        copy.start()

    @pl.when(core == 0)
    def _():
        for copy in first_only:
            copy.start()

    def text_arrived(step, h):
        remote(halves[0], text_raw.at[step, h], text_send.at[4], text_recv.at[step - 1, h], other_core).wait_recv()

    relay = remote(
        text_raw.at[1 + core, core],
        text_raw.at[2 - core, core],
        text_send.at[4],
        text_recv.at[1 - core, core],
        other_core,
    )

    for load in loads:
        load.wait()
    x_there = send(x_all.at[core], x_all.at[core], other_core)
    image_raw = dot(w_ref[...], x_all[core], 1, 1)
    sums_out[0:1, :] = jnp.sum(image_raw * image_raw, axis=0, keepdims=True)
    for h in (0, 1):
        own_text = text_raw[0, h].astype(F32)
        sums_out[1:2, h * hr : (h + 1) * hr] = jnp.sum(own_text * own_text, axis=0, keepdims=True)
    sums_there = send(sums_out, sums_in, other_mp)
    sums_there.wait_recv()
    sums = sums_out[...] + sums_in[...]
    image_scale = lax.rsqrt(sums[0:1, :] + EPSILON)
    text_scale = lax.rsqrt(sums[1:2, :] + EPSILON)
    text_sums[0] = sums
    text_sums_there = [send(text_sums.at[0], text_sums.at[s], along_dp(s)) for s in (1, 2)]
    unit = image_raw * image_scale
    image_unit[...] = unit
    image_low[...] = unit.astype(BF16)

    def cos_copy(s, h):
        return remote(cos_out.at[s, h], cos_in.at[s, h], cos_send.at[s, h], cos_recv.at[s, h], other_mp)

    def cosines(s, h):
        scale = lax.rsqrt(text_sums[s, 1:2, :] + EPSILON)
        if isinstance(h, int):
            scale = scale[:, h * hr : (h + 1) * hr]
        else:
            scale = jnp.where(h == 0, scale[:, :hr], scale[:, hr:])
        low = (text_raw[s, h].astype(F32) * scale).astype(BF16)
        text_low[s, h] = low
        cos_out[s, h] = dot(low, image_low[...], 0, 0).astype(BF16)
        cos_copy(s, h).start()

    cosines(0, 0)
    cosines(0, 1)
    for copy in text_sums_there:
        copy.wait_recv()
    units = [(1, 0), (2 - core, core), (2, 1), (1 + core, 1 - core)]
    for number, (s, h) in enumerate(units):
        text_arrived(s, h)
        if number in (0, 2):

            @pl.when(core == number // 2)
            def _():
                relay.start()

        cosines(s, h)

    sharpness, offset = scale_ref[0], offset_ref[0]
    loss_rows = jnp.zeros((1, rows), F32)
    along_unit = jnp.zeros((1, rows), F32)
    direction = jnp.zeros((width, rows), F32)
    for s, h in [(0, 0), (0, 1)] + units:
        cos_copy(s, h).wait_recv()
        cos = cos_out[s, h].astype(F32) + cos_in[s, h].astype(F32)
        first = lax.rem(dp - s + BLOCKS, BLOCKS) * rows + h * hr
        matched = first + lax.broadcasted_iota(jnp.int32, (hr, rows), 0) == matched_ref[...]
        logit = sharpness * cos + offset
        against = jnp.where(matched, -logit, logit)
        small = jnp.exp(-jnp.abs(against))
        loss_rows += jnp.sum(jnp.maximum(against, 0.0) + jnp.log1p(small), axis=0, keepdims=True)
        sigmoid = jnp.where(against >= 0.0, 1.0, small) / (1.0 + small)
        low = (jnp.where(matched, -sigmoid, sigmoid) * sharpness).astype(BF16)
        weight[s, h] = low
        along_unit += jnp.sum(low.astype(F32) * cos, axis=0, keepdims=True)
        direction += dot(text_low[s, h], low, 1, 0)

    image_back = ((direction - image_unit[...] * along_unit) * image_scale).astype(BF16)
    back[0] = image_back[:half]
    back[1] = image_back[half:]
    back_there = send(back.at[1 - core], back_all.at[core], other_core)
    back_all[core] = back[core]
    loss_core[core] = jnp.broadcast_to(loss_rows, (8, rows))
    loss_core_there = send(loss_core.at[core], loss_core.at[core], other_core)

    def text_parts(s, h):
        text_part[s - 1, h] = dot(image_low[...], weight[s, h], 1, 1).astype(BF16)

    shared, alone = 1 + core, 2 - core
    text_parts(shared, 1 - core)
    presum_there = send(text_part.at[core, 1 - core], presum_in, other_core)

    def part_copy(source, which, h, step, number):
        return remote(
            source, text_in.at[which, h], part_send.at[number], part_recv.at[which, h], along_dp(-step)
        )

    part_copies = []
    for h in (0, 1):
        text_parts(alone, h)
        part_copies.append(part_copy(text_part.at[1 - core, h], 1 - core, h, alone, h))
        part_copies[-1].start()

    x_there.wait_recv()
    back_there.wait_recv()
    mine, theirs = back_all[core], back_all[1 - core]
    x_mine, x_theirs = x_all[core], x_all[1 - core]
    groups = groups_of(width, depth)
    levels = []
    for g, (first, last, order, _, held) in enumerate(groups):
        full, sums_2, sums_3, land_1, land_2, land_3, got_3, got_2, result = buffers[9 * g : 9 * g + 9]
        levels.append(([full, sums_2, sums_3], [land_1, land_2, land_3], [result, got_2, got_3]))

    def scatter(g, level):
        _, _, order, _, held = groups[g]
        source, landing = levels[g][0][level], levels[g][1][level]
        return [
            send(rows_of(source, place, held[level + 1]), landing.at[k], device)
            for k, (place, device) in enumerate(others(order[level]))
        ]

    def scattered(g, level, there):
        _, _, order, _, held = groups[g]
        source, landing = levels[g][0][level], levels[g][1][level]
        total = rows_of(source, at[order[level]], held[level + 1])[...].astype(F32)
        for k, copy in enumerate(there):
            copy.wait_recv()
            total += landing[k].astype(F32)
        return total.astype(BF16)

    def padded(ref, count):
        if ref.shape[0] > count:
            ref[count:, :] = jnp.zeros((ref.shape[0] - count, LANES), BF16)

    def loss_spread(landing, axis, value):
        landing[at[axis]] = value
        return [send(landing.at[at[axis]], landing.at[at[axis]], device) for _, device in others(axis)]

    def loss_sum(there, landing, axis):
        for copy in there:
            copy.wait_recv()
        total = landing[0]
        for k in range(1, counts[axis]):
            total += landing[k]
        return total

    there = []
    for g, (first, last, order, _, held) in enumerate(groups):
        full = levels[g][0][0]
        for k in range(first, last):
            cols = slice(k * LANES, (k + 1) * LANES)
            part = dot(mine, x_mine[:, cols], 1, 0) + dot(theirs, x_theirs[:, cols], 1, 0)
            full[(k - first) * half : (k - first + 1) * half, :] = part.astype(BF16)
        padded(full, held[0])
        there.append(scatter(g, 0))
    loss_core_there.wait_recv()
    loss_there = loss_spread(loss_x, "x", loss_core[0] + loss_core[1])

    text_parts(shared, core)
    for h in (0, 1):
        text_dir[h] = dot(image_low[...], weight[0, h], 1, 1)
    presum_there.wait_recv()
    presum_out[...] = (text_part[core, core].astype(F32) + presum_in[...].astype(F32)).astype(BF16)
    part_copies.append(part_copy(presum_out, 0, core, shared, 2))
    part_copies[-1].start()

    for level in range(3):
        for g, (_, _, order, _, held) in enumerate(groups):
            total = scattered(g, level, there[g])
            if level < 2:
                target = levels[g][0][level + 1]
                target[: held[level + 1], :] = total
                padded(target, held[level + 1])
                there[g] = scatter(g, level + 1)
            else:
                own = rows_of(levels[g][2][2], at[order[2]], held[3])
                own[...] = total
                there[g] = [send(own, own, device) for _, device in others(order[2])]
        if level == 0:
            loss_there = loss_spread(loss_y, "y", loss_sum(loss_there, loss_x, "x"))
        if level == 1:
            loss_there = loss_spread(loss_z, "z", loss_sum(loss_there, loss_y, "y"))

    loss_now = loss_sum(loss_there, loss_z, "z")
    loss_ref[0] = jnp.sum(loss_now[0:1, :]) / (rows * BLOCKS)

    def part_arrived(which, h):
        part_copy(presum_out, which, h, 1, 2).wait_recv()

    for h in (0, 1):
        part_arrived(0, h)
        text_dir[h] += text_in[0, h].astype(F32)

    @pl.when(core == 0)
    def _():
        for h in (0, 1):
            part_arrived(1, h)
            text_dir[h] += text_in[1, h].astype(F32)

    def text_unit(h):
        return text_raw[0, h].astype(F32) * text_scale[:, h * hr : (h + 1) * hr]

    for h in (0, 1):
        tdot_out[:, h * hr : (h + 1) * hr] = jnp.broadcast_to(
            jnp.sum(text_unit(h) * text_dir[h], axis=0, keepdims=True), (8, hr)
        )
    tdot_there = send(tdot_out, tdot_in, other_mp)

    for g, (_, _, order, _, held) in enumerate(groups):
        for copy in there[g]:
            copy.wait_recv()
        own = rows_of(levels[g][2][1], at[order[1]], held[2])
        own[...] = levels[g][2][2][: held[2], :]
        there[g] = [send(own, own, device) for _, device in others(order[1])]

    tdot_there.wait_recv()
    tdot = tdot_out[0:1, :] + tdot_in[0:1, :]
    for h in (0, 1):
        lanes = slice(h * hr, (h + 1) * hr)
        cap_ref[:, lanes] = (
            (text_dir[h] - text_unit(h) * tdot[:, lanes]) * text_scale[:, lanes]
        ).astype(BF16)

    def chunk(g, place):
        return rows_of(levels[g][2][0].at[core], place, groups[g][4][1])

    relayed = []
    for g, (_, _, order, _, held) in enumerate(groups):
        for copy in there[g]:
            copy.wait_recv()
        own = chunk(g, at[order[0]])
        own[...] = levels[g][2][1][: held[1], :]
        there[g] = [send(own, own, device) for _, device in others(order[0])]
        relayed.append(send(own, own, other_core))
    for g, (_, _, order, _, held) in enumerate(groups):
        for k, copy in enumerate(there[g]):
            copy.wait_recv()
            arrived = chunk(g, source_of(order[0], k + 1))
            relayed.append(send(arrived, arrived, other_core))
    for copy in relayed:
        copy.wait_recv()
    for g, (first, last, _, _, _) in enumerate(groups):
        result = levels[g][2][0]
        for c in range(2):
            for k in range(first, last):
                rows_k = slice((k - first) * half, (k - first + 1) * half)
                grad_ref[c * half : (c + 1) * half, k * LANES : (k + 1) * LANES] = result[c, rows_k, :]

    for copy in copies.made + both + [relay] + part_copies:
        copy.wait_send()

    @pl.when(core == 0)
    def _():
        for copy in first_only:
            copy.wait_send()

    for s in range(STEPS + 1):
        for h in (0, 1):
            cos_copy(s, h).wait_send()


def local(x_rows, w_half, t_half, matched, sharpness, offset):
    rows, depth = x_rows.shape
    width = w_half.shape[1]
    half, hr = width // 2, rows // 2
    vmem, hbm = pl.BlockSpec(memory_space=pltpu.VMEM), pl.BlockSpec(memory_space=pltpu.HBM)
    smem = pl.BlockSpec(memory_space=pltpu.SMEM)
    buffers = []
    for _, _, _, (n1, n2, n3), (_, r1, r2, r3) in groups_of(width, depth):
        buffers += [
            pltpu.VMEM((n1 * r1, LANES), BF16),
            pltpu.VMEM((n2 * r2, LANES), BF16),
            pltpu.VMEM((n3 * r3, LANES), BF16),
            pltpu.VMEM((n1 - 1, r1, LANES), BF16),
            pltpu.VMEM((n2 - 1, r2, LANES), BF16),
            pltpu.VMEM((n3 - 1, r3, LANES), BF16),
            pltpu.VMEM((n3 * r3, LANES), BF16),
            pltpu.VMEM((n2 * r2, LANES), BF16),
            pltpu.VMEM((2, n1 * r1, LANES), BF16),
        ]
    call = pl.pallas_call(
        kernel,
        out_shape=(
            jax.ShapeDtypeStruct((1,), F32),
            jax.ShapeDtypeStruct((width, depth), BF16),
            jax.ShapeDtypeStruct((width, rows), BF16),
        ),
        in_specs=[hbm, hbm, hbm, vmem, smem, smem],
        out_specs=(smem, vmem, vmem),
        scratch_shapes=[
            pltpu.VMEM((2, rows, depth), BF16),
            pltpu.VMEM((width, depth), BF16),
            pltpu.VMEM((3, 2, width, hr), BF16),
            pltpu.VMEM((3, 2, width, hr), BF16),
            pltpu.VMEM((width, rows), F32),
            pltpu.VMEM((width, rows), BF16),
            pltpu.VMEM((8, rows), F32),
            pltpu.VMEM((8, rows), F32),
            pltpu.VMEM((3, 8, rows), F32),
            pltpu.VMEM((3, 2, hr, rows), BF16),
            pltpu.VMEM((3, 2, hr, rows), BF16),
            pltpu.VMEM((3, 2, hr, rows), BF16),
            pltpu.VMEM((2, half, rows), BF16),
            pltpu.VMEM((2, half, rows), BF16),
            pltpu.VMEM((2, 8, rows), F32),
            pltpu.VMEM((NX, 8, rows), F32),
            pltpu.VMEM((NY, 8, rows), F32),
            pltpu.VMEM((NZ, 8, rows), F32),
            pltpu.VMEM((2, width, hr), F32),
            pltpu.VMEM((2, 2, width, hr), BF16),
            pltpu.VMEM((width, hr), BF16),
            pltpu.VMEM((width, hr), BF16),
            pltpu.VMEM((2, 2, width, hr), BF16),
            pltpu.VMEM((8, rows), F32),
            pltpu.VMEM((8, rows), F32),
            *buffers,
            pltpu.SemaphoreType.DMA((4,)),
            pltpu.SemaphoreType.DMA((5,)),
            pltpu.SemaphoreType.DMA((2, 2)),
            pltpu.SemaphoreType.DMA((3, 2)),
            pltpu.SemaphoreType.DMA((3, 2)),
            pltpu.SemaphoreType.DMA((3,)),
            pltpu.SemaphoreType.DMA((2, 2)),
            pltpu.SemaphoreType.DMA((N_COPIES,)),
            pltpu.SemaphoreType.DMA((N_COPIES,)),
        ],
        compiler_params=pltpu.CompilerParams(
            collective_id=0, has_side_effects=True, vmem_limit_bytes=40 * 1024 * 1024
        ),
    )
    loss, grad, cap = call(x_rows, w_half.T, t_half.T, matched.reshape(1, rows), sharpness, offset)
    return (loss, grad.T, cap.T)


def solution(mesh):
    placed = (P("dp", None), P(None, "mp"), P("dp", "mp"), P("dp"), P(), P())
    return jax.shard_map(
        local,
        mesh=mesh,
        in_specs=placed,
        out_specs=(P(), P(None, "mp"), P("dp", "mp")),
        check_vma=False,
    )
```

time: 111 us -> 93.8 us (0.85)
  the two profiles are of different devices: /device:TPU:21 before, /device:TPU:1 now
where the time goes in v2:
time: 93.8 us; the launch traced here: 93.5 us
  Pallas kernels  84.1 us (90%)
  local copies, waits for them, and re-layouts  5.8 us (6%)
  between operations  3.69 us (4%)
    pallas_call x1, Pallas kernels, local(): call(x_rows, w_half.T, t_half.T, matched.reshape(1, rows), sharpness, off...  84.1 us
    unnamed x10, local copies, waits for them, and re-layouts  5.8 us

profile of v2, /device:TPU:1, one launch (start us, length us, event | category | flops | bytes accessed | tf_op | source)
XLA Modules:
  0.0 93.5 jit_solution(6792655989544334261)
XLA Ops:
  1.9 0.0 copy-start
  1.9 1.3 %copy-done = bf16[1152,576]{0,1:T(8,128)(2,1)S(1)} copy-done((bf16[1152,576]{0,1:T(8,128)(2,1)S(1)}, bf16[1152,576]{0,1:T(8,128)(2,1)}, u32[]{:S(2)}) %copy-start) | copy-done | bytes 1327128
  3.2 0.0 copy-start.1
  3.2 1.1 %copy-done.1 = bf16[256,1152]{1,0:T(8,128)(2,1)S(1)} copy-done((bf16[256,1152]{1,0:T(8,128)(2,1)S(1)}, bf16[256,1152]{1,0:T(8,128)(2,1)}, u32[]{:S(2)}) %copy-start.1) | copy-done | bytes 589848
  4.3 0.0 copy-start.2
  4.3 1.0 %copy-done.2 = bf16[256,576]{0,1:T(8,128)(2,1)S(1)} copy-done((bf16[256,576]{0,1:T(8,128)(2,1)S(1)}, bf16[256,576]{0,1:T(8,128)(2,1)}, u32[]{:S(2)}) %copy-start.2) | copy-done | bytes 294936
  5.3 0.0 copy-start.3
  5.3 0.7 copy-done.3
  6.0 84.1 %shard_map.85 = (f32[1]{0:T(128)}, bf16[576,1152]{1,0:T(8,128)(2,1)S(1)}, bf16[576,256]{1,0:T(8,128)(2,1)S(1)}) custom-call(bf16[256,1152]{1,0:T(8,128)(2,1)S(1)} %copy-done.1, bf16[576,1152]{1,0:T(8,128)(2,1)S(1)} %bitcast.5, bf16[576,256]{1,0:T(8,128)(2,1)S(1)} %bitcast.7, s32[1,256]{1,0:T(1,128)S(1)} %bitcast.9, f32[1]{0:T(128)S(6)} %copy.12.scale_ref, ...), custom_call_target="tpu_custom_call" | custom-call | tf_op jit(solution)/shard_map/pallas_call | solution.py:492
  90.6 1.1 %copy.15 = bf16[1152,576]{0,1:T(8,128)(2,1)} copy(bf16[1152,576]{0,1:T(8,128)(2,1)S(1)} %bitcast.6) | data formatting | bytes 2654208
  91.7 0.7 copy.16
Async XLA Ops:
  1.9 1.3 %copy-start = (bf16[1152,576]{0,1:T(8,128)(2,1)S(1)}, bf16[1152,576]{0,1:T(8,128)(2,1)}, u32[]{:S(2)}) copy-start(bf16[1152,576]{0,1:T(8,128)(2,1)} %param.7) | copy-start | bytes 3981316
  3.2 1.1 %copy-start.1 = (bf16[256,1152]{1,0:T(8,128)(2,1)S(1)}, bf16[256,1152]{1,0:T(8,128)(2,1)}, u32[]{:S(2)}) copy-start(bf16[256,1152]{1,0:T(8,128)(2,1)} %x_hbm.1) | copy-start | bytes 1769476
  4.3 1.0 %copy-start.2 = (bf16[256,576]{0,1:T(8,128)(2,1)S(1)}, bf16[256,576]{0,1:T(8,128)(2,1)}, u32[]{:S(2)}) copy-start(bf16[256,576]{0,1:T(8,128)(2,1)} %param.8) | copy-start | bytes 884740
  5.3 0.7 copy-start.3

commit v3 on v2

--- a/solution.py
+++ b/solution.py
@@ -22,12 +22,12 @@
 
 def groups_of(width, depth):
     half, tiles = width // 2, depth // LANES
-    cut = tiles * 2 // 3
+    one, two = tiles * 6 // 9, tiles * 7 // 9
     groups = []
-    for first, last, order in ((0, cut, "xyz"), (cut, tiles, "yxz")):
+    for first, last, order in ((0, one, "xyz"), (one, two, "yxz"), (two, tiles, "zxy")):
         counts = [{"x": NX, "y": NY, "z": NZ}[axis] for axis in order]
         held = [(last - first) * half]
-        for count in counts:
+        for count in counts[:2]:
             held.append(-(-held[-1] // (count * ROW_TILE)) * ROW_TILE)
         groups.append((first, last, order, counts, held))
     return groups
@@ -97,7 +97,7 @@
     tdot_in,
     *rest,
 ):
-    *buffers, load_sem, text_send, text_recv, cos_send, cos_recv, part_send, part_recv, send_sem, recv_sem = rest
+    *buffers, grad_own, passed, passed_send, passed_recv, load_sem, text_send, text_recv, cos_send, cos_recv, part_send, part_recv, send_sem, recv_sem = rest
     width, rows = t_hbm.shape
     depth = x_hbm.shape[1]
     half, hr = width // 2, rows // 2
@@ -110,7 +110,7 @@
     other_core = (dp + 1 - 2 * core, mp)
 
     def along_dp(step):
-        return (lax.rem(dp + step + BLOCKS, BLOCKS), mp)
+        return (lax.rem(dp + step + 2 * BLOCKS, BLOCKS), mp)
 
     def others(axis):
         places = [lax.rem(at[axis] + k, counts[axis]) for k in range(1, counts[axis])]
@@ -119,10 +119,10 @@
     def source_of(axis, k):
         return lax.rem(at[axis] - k + counts[axis], counts[axis])
 
-    halves = [t_hbm.at[:, :hr], t_hbm.at[:, hr:]]
+    halves = [text_raw.at[0, 0], text_raw.at[0, 1]]
     loads = [
-        pltpu.make_async_copy(halves[0], text_raw.at[0, 0], load_sem.at[0]),
-        pltpu.make_async_copy(halves[1], text_raw.at[0, 1], load_sem.at[1]),
+        pltpu.make_async_copy(t_hbm.at[:, :hr], text_raw.at[0, 0], load_sem.at[0]),
+        pltpu.make_async_copy(t_hbm.at[:, hr:], text_raw.at[0, 1], load_sem.at[1]),
         pltpu.make_async_copy(w_hbm, w_ref, load_sem.at[2]),
         pltpu.make_async_copy(x_hbm, x_all.at[core], load_sem.at[3]),
     ]
@@ -134,7 +134,37 @@
     greeted += [device for axis in "xyz" for _, device in others(axis)]
     for device in greeted:
         pl.semaphore_signal(barrier, inc=1, device_id=device, device_id_type=MESH)
-    pl.semaphore_wait(barrier, len(greeted))
+
+    chip, plane = 2 * NX, 2 * NX * NY
+    corner = (at["x"] == NX - 1) & (at["y"] == NY - 1)
+    landing = (at["x"] == 0) & (at["y"] == 0)
+    via_z = corner & (core == 1)
+    via_x = (at["x"] == 0) & (at["y"] == NY - 1) & (core == 0)
+    via_y = (at["x"] == NX - 1) & (at["y"] == 1) & (core == 0)
+    passes_on = via_z | via_x | via_y
+    back_z, back_x, back_y = -plane, 2 * (NX - 1), (NY - 2) * chip - plane
+    back_here = jnp.where(via_z, back_z, jnp.where(via_x, back_x, back_y))
+
+    def greet(device):
+        pl.semaphore_signal(barrier, inc=1, device_id=device, device_id_type=MESH)
+
+    @pl.when(passes_on)
+    def _():
+        greet(along_dp(back_here))
+
+    @pl.when(landing & (core == 0))
+    def _():
+        greet(along_dp(-2 - back_x))
+        greet(along_dp(-2 - back_y))
+
+    @pl.when(landing & (core == 1))
+    def _():
+        greet(along_dp(-2 - back_z))
+
+    more = jnp.where(passes_on, 1, 0) + jnp.where(corner, 2 - core, 0)
+    for load in loads[:2]:
+        load.wait()
+    pl.semaphore_wait(barrier, len(greeted) + more)
 
     copies = Copies(send_sem, recv_sem)
     send = copies.start
@@ -148,15 +178,43 @@
             along_dp(step),
         )
 
-    both = [text_copy(0, 1, 0), text_copy(1, 2, 1)]
-    first_only = [text_copy(0, 2, 2), text_copy(1, 1, 3)]
-    for copy in both:
-        copy.start()
-
-    @pl.when(core == 0)
-    def _():
-        for copy in first_only:
-            copy.start()
+    def text_away(h, back, number):
+        return remote(halves[h], passed, text_send.at[number], passed_recv.at[0], along_dp(-back))
+
+    straight = ~corner
+
+    @pl.when((core == 1) | straight)
+    def _():
+        text_copy(0, 1, 0).start()
+
+    @pl.when(straight)
+    def _():
+        text_copy(1, 2, 1).start()
+
+    @pl.when((core == 0) & straight)
+    def _():
+        text_copy(0, 2, 2).start()
+        text_copy(1, 1, 3).start()
+
+    @pl.when((core == 1) & corner)
+    def _():
+        text_away(1, back_z, 1).start()
+
+    @pl.when((core == 0) & corner)
+    def _():
+        text_away(0, back_x, 2).start()
+        text_away(1, back_y, 1).start()
+        text_copy(0, 1, 0).start()
+        text_copy(1, 1, 3).start()
+
+    pass_half = jnp.where(via_x, 0, 1)
+    pass_on = remote(
+        passed,
+        text_raw.at[2, pass_half],
+        passed_send.at[0],
+        text_recv.at[1, pass_half],
+        along_dp(back_here + 2),
+    )
 
     def text_arrived(step, h):
         remote(halves[0], text_raw.at[step, h], text_send.at[4], text_recv.at[step - 1, h], other_core).wait_recv()
@@ -169,7 +227,7 @@
         other_core,
     )
 
-    for load in loads:
+    for load in loads[2:]:
         load.wait()
     x_there = send(x_all.at[core], x_all.at[core], other_core)
     image_raw = dot(w_ref[...], x_all[core], 1, 1)
@@ -178,6 +236,12 @@
         own_text = text_raw[0, h].astype(F32)
         sums_out[1:2, h * hr : (h + 1) * hr] = jnp.sum(own_text * own_text, axis=0, keepdims=True)
     sums_there = send(sums_out, sums_in, other_mp)
+
+    @pl.when(passes_on)
+    def _():
+        remote(halves[0], passed, passed_send.at[0], passed_recv.at[0], other_core).wait_recv()
+        pass_on.start()
+
     sums_there.wait_recv()
     sums = sums_out[...] + sums_in[...]
     image_scale = lax.rsqrt(sums[0:1, :] + EPSILON)
@@ -248,29 +312,20 @@
         text_part[s - 1, h] = dot(image_low[...], weight[s, h], 1, 1).astype(BF16)
 
     shared, alone = 1 + core, 2 - core
-    text_parts(shared, 1 - core)
-    presum_there = send(text_part.at[core, 1 - core], presum_in, other_core)
-
     def part_copy(source, which, h, step, number):
         return remote(
             source, text_in.at[which, h], part_send.at[number], part_recv.at[which, h], along_dp(-step)
         )
 
-    part_copies = []
-    for h in (0, 1):
-        text_parts(alone, h)
-        part_copies.append(part_copy(text_part.at[1 - core, h], 1 - core, h, alone, h))
-        part_copies[-1].start()
-
+    grad_own[...] = dot(back_all[core], x_all[core], 1, 0)
     x_there.wait_recv()
     back_there.wait_recv()
-    mine, theirs = back_all[core], back_all[1 - core]
-    x_mine, x_theirs = x_all[core], x_all[1 - core]
+    theirs, x_theirs = back_all[1 - core], x_all[1 - core]
     groups = groups_of(width, depth)
     levels = []
     for g, (first, last, order, _, held) in enumerate(groups):
-        full, sums_2, sums_3, land_1, land_2, land_3, got_3, got_2, result = buffers[9 * g : 9 * g + 9]
-        levels.append(([full, sums_2, sums_3], [land_1, land_2, land_3], [result, got_2, got_3]))
+        full, sums_2, land_1, land_2, land_3, got_2, result = buffers[7 * g : 7 * g + 7]
+        levels.append(([full, sums_2], [land_1, land_2, land_3], [result, got_2]))
 
     def scatter(g, level):
         _, _, order, _, held = groups[g]
@@ -293,7 +348,7 @@
         if ref.shape[0] > count:
             ref[count:, :] = jnp.zeros((ref.shape[0] - count, LANES), BF16)
 
-    def loss_spread(landing, axis, value):
+    def spread(landing, axis, value):
         landing[at[axis]] = value
         return [send(landing.at[at[axis]], landing.at[at[axis]], device) for _, device in others(axis)]
 
@@ -310,37 +365,47 @@
         full = levels[g][0][0]
         for k in range(first, last):
             cols = slice(k * LANES, (k + 1) * LANES)
-            part = dot(mine, x_mine[:, cols], 1, 0) + dot(theirs, x_theirs[:, cols], 1, 0)
+            part = grad_own[:, cols] + dot(theirs, x_theirs[:, cols], 1, 0)
             full[(k - first) * half : (k - first + 1) * half, :] = part.astype(BF16)
         padded(full, held[0])
         there.append(scatter(g, 0))
     loss_core_there.wait_recv()
-    loss_there = loss_spread(loss_x, "x", loss_core[0] + loss_core[1])
-
+    loss_there = spread(loss_x, "x", loss_core[0] + loss_core[1])
+
+    text_parts(shared, 1 - core)
+    presum_there = send(text_part.at[core, 1 - core], presum_in, other_core)
     text_parts(shared, core)
+    for h in (0, 1):
+        text_parts(alone, h)
     for h in (0, 1):
         text_dir[h] = dot(image_low[...], weight[0, h], 1, 1)
     presum_there.wait_recv()
     presum_out[...] = (text_part[core, core].astype(F32) + presum_in[...].astype(F32)).astype(BF16)
-    part_copies.append(part_copy(presum_out, 0, core, shared, 2))
-    part_copies[-1].start()
-
-    for level in range(3):
-        for g, (_, _, order, _, held) in enumerate(groups):
-            total = scattered(g, level, there[g])
-            if level < 2:
-                target = levels[g][0][level + 1]
-                target[: held[level + 1], :] = total
-                padded(target, held[level + 1])
-                there[g] = scatter(g, level + 1)
-            else:
-                own = rows_of(levels[g][2][2], at[order[2]], held[3])
-                own[...] = total
-                there[g] = [send(own, own, device) for _, device in others(order[2])]
-        if level == 0:
-            loss_there = loss_spread(loss_y, "y", loss_sum(loss_there, loss_x, "x"))
-        if level == 1:
-            loss_there = loss_spread(loss_z, "z", loss_sum(loss_there, loss_y, "y"))
+    part_copies = [
+        part_copy(text_part.at[1 - core, h], 1 - core, h, alone, h) for h in (0, 1)
+    ] + [part_copy(presum_out, 0, core, shared, 2)]
+
+    for g, (_, _, order, _, held) in enumerate(groups):
+        target = levels[g][0][1]
+        target[: held[1], :] = scattered(g, 0, there[g])
+        padded(target, held[1])
+        there[g] = scatter(g, 1)
+    loss_there = spread(loss_y, "y", loss_sum(loss_there, loss_x, "x"))
+    for copy in part_copies:
+        copy.start()
+    for g, (_, _, order, _, held) in enumerate(groups):
+        there[g] = spread(levels[g][1][2], order[2], scattered(g, 1, there[g]))
+    loss_there = spread(loss_z, "z", loss_sum(loss_there, loss_y, "y"))
+    for g, (_, _, order, counts_g, held) in enumerate(groups):
+        landing_g = levels[g][1][2]
+        for copy in there[g]:
+            copy.wait_recv()
+        total = landing_g[0].astype(F32)
+        for k in range(1, counts_g[2]):
+            total += landing_g[k].astype(F32)
+        own = rows_of(levels[g][2][1], at[order[1]], held[2])
+        own[...] = total.astype(BF16)
+        there[g] = [send(own, own, device) for _, device in others(order[1])]
 
     loss_now = loss_sum(loss_there, loss_z, "z")
     loss_ref[0] = jnp.sum(loss_now[0:1, :]) / (rows * BLOCKS)
@@ -366,13 +431,6 @@
             jnp.sum(text_unit(h) * text_dir[h], axis=0, keepdims=True), (8, hr)
         )
     tdot_there = send(tdot_out, tdot_in, other_mp)
-
-    for g, (_, _, order, _, held) in enumerate(groups):
-        for copy in there[g]:
-            copy.wait_recv()
-        own = rows_of(levels[g][2][1], at[order[1]], held[2])
-        own[...] = levels[g][2][2][: held[2], :]
-        there[g] = [send(own, own, device) for _, device in others(order[1])]
 
     tdot_there.wait_recv()
     tdot = tdot_out[0:1, :] + tdot_in[0:1, :]
@@ -407,13 +465,17 @@
                 rows_k = slice((k - first) * half, (k - first + 1) * half)
                 grad_ref[c * half : (c + 1) * half, k * LANES : (k + 1) * LANES] = result[c, rows_k, :]
 
-    for copy in copies.made + both + [relay] + part_copies:
+    for copy in copies.made + [text_copy(0, 1, 0), text_copy(1, 2, 1), relay] + part_copies:
         copy.wait_send()
 
     @pl.when(core == 0)
     def _():
-        for copy in first_only:
+        for copy in (text_copy(0, 2, 2), text_copy(1, 1, 3)):
             copy.wait_send()
+
+    @pl.when(passes_on)
+    def _():
+        pass_on.wait_send()
 
     for s in range(STEPS + 1):
         for h in (0, 1):
@@ -427,15 +489,13 @@
     vmem, hbm = pl.BlockSpec(memory_space=pltpu.VMEM), pl.BlockSpec(memory_space=pltpu.HBM)
     smem = pl.BlockSpec(memory_space=pltpu.SMEM)
     buffers = []
-    for _, _, _, (n1, n2, n3), (_, r1, r2, r3) in groups_of(width, depth):
+    for _, _, _, (n1, n2, n3), (_, r1, r2) in groups_of(width, depth):
         buffers += [
             pltpu.VMEM((n1 * r1, LANES), BF16),
             pltpu.VMEM((n2 * r2, LANES), BF16),
-            pltpu.VMEM((n3 * r3, LANES), BF16),
             pltpu.VMEM((n1 - 1, r1, LANES), BF16),
             pltpu.VMEM((n2 - 1, r2, LANES), BF16),
-            pltpu.VMEM((n3 - 1, r3, LANES), BF16),
-            pltpu.VMEM((n3 * r3, LANES), BF16),
+            pltpu.VMEM((n3, r2, LANES), BF16),
             pltpu.VMEM((n2 * r2, LANES), BF16),
             pltpu.VMEM((2, n1 * r1, LANES), BF16),
         ]
@@ -475,6 +535,10 @@
             pltpu.VMEM((8, rows), F32),
             pltpu.VMEM((8, rows), F32),
             *buffers,
+            pltpu.VMEM((half, depth), F32),
+            pltpu.VMEM((width, hr), BF16),
+            pltpu.SemaphoreType.DMA((1,)),
+            pltpu.SemaphoreType.DMA((1,)),
             pltpu.SemaphoreType.DMA((4,)),
             pltpu.SemaphoreType.DMA((5,)),
             pltpu.SemaphoreType.DMA((2, 2)),
@@ -486,7 +550,7 @@
             pltpu.SemaphoreType.DMA((N_COPIES,)),
         ],
         compiler_params=pltpu.CompilerParams(
-            collective_id=0, has_side_effects=True, vmem_limit_bytes=40 * 1024 * 1024
+            collective_id=0, has_side_effects=True, vmem_limit_bytes=56 * 1024 * 1024
         ),
     )
     loss, grad, cap = call(x_rows, w_half.T, t_half.T, matched.reshape(1, rows), sharpness, offset)

time: 93.8 us -> 85.3 us (0.909)
  Pallas kernels: 84.1 us -> 78.1 us
  local copies, waits for them, and re-layouts: 5.8 us -> 3.25 us
    pallas_call x1, Pallas kernels: 84.1 us -> 78.1 us  [local(): call(x_rows, w_half.T, t_half.T, matched.reshape(1, rows), sharpness, off...]
    unnamed x10 -> x4, local copies, waits for them, and re-layouts: 5.8 us -> 3.25 us
where the time goes in v3:
time: 85.3 us; the launch traced here: 85.1 us
  Pallas kernels  78.1 us (92%)
  between operations  3.76 us (4%)
  local copies, waits for them, and re-layouts  3.25 us (4%)
    pallas_call x1, Pallas kernels, local(): call(x_rows, w_half.T, t_half.T, matched.reshape(1, rows), sharpness, off...  78.1 us
    unnamed x4, local copies, waits for them, and re-layouts  3.25 us

profile of v3, /device:TPU:1, one launch (start us, length us, event | category | flops | bytes accessed | tf_op | source)
XLA Modules:
  0.0 85.1 jit_solution(17890534253389405835)
XLA Ops:
  1.9 78.1 %shard_map.85 = (f32[1]{0:T(128)}, bf16[576,1152]{1,0:T(8,128)(2,1)}, bf16[576,256]{1,0:T(8,128)(2,1)}) custom-call(bf16[256,1152]{1,0:T(8,128)(2,1)} %x_hbm.1, bf16[576,1152]{1,0:T(8,128)(2,1)} %bitcast.5, bf16[576,256]{1,0:T(8,128)(2,1)} %bitcast.7, s32[1,256]{1,0:T(1,128)} %bitcast.9, f32[1]{0:T(128)S(6)} %copy.12.scale_ref, f32[1]{0:T(128)S(6)} %copy.13.offset_ref), custom_call_target="tpu_custom_call" | custom-call | tf_op jit(solution)/shard_map/pallas_call | solution.py:556
  80.7 0.0 copy-start
  80.7 2.5 %copy.15 = bf16[1152,576]{0,1:T(8,128)(2,1)} copy(bf16[1152,576]{0,1:T(8,128)(2,1)} %bitcast.6) | data formatting | bytes 2654208
  83.2 0.0 copy-done
  83.3 0.7 copy.16
Async XLA Ops:
  80.7 2.5 %copy-start = (bf16[576,256]{1,0:T(8,128)(2,1)S(1)}, bf16[576,256]{1,0:T(8,128)(2,1)}, u32[]{:S(2)}) copy-start(bf16[576,256]{1,0:T(8,128)(2,1)} %get-tuple-element.8) | copy-start | bytes 884740

commit v4 on v3

--- a/solution.py
+++ b/solution.py
@@ -22,7 +22,7 @@
 
 def groups_of(width, depth):
     half, tiles = width // 2, depth // LANES
-    one, two = tiles * 6 // 9, tiles * 7 // 9
+    one, two = tiles * 4 // 9, tiles * 7 // 9
     groups = []
     for first, last, order in ((0, one, "xyz"), (one, two, "yxz"), (two, tiles, "zxy")):
         counts = [{"x": NX, "y": NY, "z": NZ}[axis] for axis in order]
@@ -64,12 +64,12 @@
     x_hbm,
     w_hbm,
     t_hbm,
-    matched_ref,
-    scale_ref,
-    offset_ref,
+    matched_hbm,
+    scale_hbm,
+    offset_hbm,
     loss_ref,
-    grad_ref,
-    cap_ref,
+    grad_hbm,
+    cap_hbm,
     x_all,
     w_ref,
     text_raw,
@@ -97,7 +97,7 @@
     tdot_in,
     *rest,
 ):
-    *buffers, grad_own, passed, passed_send, passed_recv, load_sem, text_send, text_recv, cos_send, cos_recv, part_send, part_recv, send_sem, recv_sem = rest
+    *buffers, cap_out, out_sem, grad_own, matched_ref, scale_ref, offset_ref, passed, passed_send, passed_recv, load_sem, text_send, text_recv, cos_send, cos_recv, part_send, part_recv, send_sem, recv_sem = rest
     width, rows = t_hbm.shape
     depth = x_hbm.shape[1]
     half, hr = width // 2, rows // 2
@@ -125,6 +125,9 @@
         pltpu.make_async_copy(t_hbm.at[:, hr:], text_raw.at[0, 1], load_sem.at[1]),
         pltpu.make_async_copy(w_hbm, w_ref, load_sem.at[2]),
         pltpu.make_async_copy(x_hbm, x_all.at[core], load_sem.at[3]),
+        pltpu.make_async_copy(matched_hbm, matched_ref, load_sem.at[4]),
+        pltpu.make_async_copy(scale_hbm, scale_ref, load_sem.at[5]),
+        pltpu.make_async_copy(offset_hbm, offset_ref, load_sem.at[6]),
     ]
     for load in loads:
         load.start()
@@ -161,7 +164,27 @@
     def _():
         greet(along_dp(-2 - back_z))
 
+    home_z = landing & (core == 1)
+    home_x = (at["x"] == NX - 1) & (at["y"] == 0) & (core == 0)
+    home_y = (at["x"] == 0) & (at["y"] == NY - 2) & (core == 0)
+    passes_home = home_z | home_x | home_y
+    from_here = -jnp.where(home_z, back_z, jnp.where(home_x, back_x, back_y))
+
+    @pl.when(passes_home)
+    def _():
+        greet(along_dp(from_here))
+
+    @pl.when(corner & (core == 0))
+    def _():
+        greet(along_dp(2 + back_x))
+        greet(along_dp(2 + back_y))
+
+    @pl.when(corner & (core == 1))
+    def _():
+        greet(along_dp(2 + back_z))
+
     more = jnp.where(passes_on, 1, 0) + jnp.where(corner, 2 - core, 0)
+    more += jnp.where(passes_home, 1, 0) + jnp.where(landing, 2 - core, 0)
     for load in loads[:2]:
         load.wait()
     pl.semaphore_wait(barrier, len(greeted) + more)
@@ -391,11 +414,44 @@
         padded(target, held[1])
         there[g] = scatter(g, 1)
     loss_there = spread(loss_y, "y", loss_sum(loss_there, loss_x, "x"))
-    for copy in part_copies:
-        copy.start()
+
+    def part_away(source, back, number):
+        return remote(source, passed, part_send.at[number], passed_recv.at[0], along_dp(back))
+
+    @pl.when(~landing)
+    def _():
+        for copy in part_copies:
+            copy.start()
+
+    @pl.when(landing & (core == 0))
+    def _():
+        part_away(text_part.at[1, 0], back_x, 0).start()
+        part_away(text_part.at[1, 1], back_y, 1).start()
+        part_copies[2].start()
+
+    @pl.when(landing & (core == 1))
+    def _():
+        part_copies[0].start()
+        part_copies[1].start()
+        part_away(presum_out, back_z, 2).start()
+
+    home_which, home_half = jnp.where(home_z, 0, 1), jnp.where(home_x, 0, 1)
+    pass_home = remote(
+        passed,
+        text_in.at[home_which, home_half],
+        passed_send.at[0],
+        part_recv.at[home_which, home_half],
+        along_dp(from_here - 2),
+    )
     for g, (_, _, order, _, held) in enumerate(groups):
         there[g] = spread(levels[g][1][2], order[2], scattered(g, 1, there[g]))
     loss_there = spread(loss_z, "z", loss_sum(loss_there, loss_y, "y"))
+
+    @pl.when(passes_home)
+    def _():
+        remote(presum_out, passed, passed_send.at[0], passed_recv.at[0], other_core).wait_recv()
+        pass_home.start()
+
     for g, (_, _, order, counts_g, held) in enumerate(groups):
         landing_g = levels[g][1][2]
         for copy in there[g]:
@@ -410,60 +466,72 @@
     loss_now = loss_sum(loss_there, loss_z, "z")
     loss_ref[0] = jnp.sum(loss_now[0:1, :]) / (rows * BLOCKS)
 
-    def part_arrived(which, h):
-        part_copy(presum_out, which, h, 1, 2).wait_recv()
-
-    for h in (0, 1):
-        part_arrived(0, h)
-        text_dir[h] += text_in[0, h].astype(F32)
-
-    @pl.when(core == 0)
-    def _():
-        for h in (0, 1):
-            part_arrived(1, h)
-            text_dir[h] += text_in[1, h].astype(F32)
-
-    def text_unit(h):
-        return text_raw[0, h].astype(F32) * text_scale[:, h * hr : (h + 1) * hr]
-
-    for h in (0, 1):
-        tdot_out[:, h * hr : (h + 1) * hr] = jnp.broadcast_to(
-            jnp.sum(text_unit(h) * text_dir[h], axis=0, keepdims=True), (8, hr)
-        )
-    tdot_there = send(tdot_out, tdot_in, other_mp)
-
-    tdot_there.wait_recv()
-    tdot = tdot_out[0:1, :] + tdot_in[0:1, :]
-    for h in (0, 1):
-        lanes = slice(h * hr, (h + 1) * hr)
-        cap_ref[:, lanes] = (
-            (text_dir[h] - text_unit(h) * tdot[:, lanes]) * text_scale[:, lanes]
-        ).astype(BF16)
-
     def chunk(g, place):
         return rows_of(levels[g][2][0].at[core], place, groups[g][4][1])
 
-    relayed = []
+    relayed = [[] for _ in groups]
     for g, (_, _, order, _, held) in enumerate(groups):
         for copy in there[g]:
             copy.wait_recv()
         own = chunk(g, at[order[0]])
         own[...] = levels[g][2][1][: held[1], :]
         there[g] = [send(own, own, device) for _, device in others(order[0])]
-        relayed.append(send(own, own, other_core))
+        relayed[g].append(send(own, own, other_core))
+
+    def part_arrived(which, h):
+        part_copy(presum_out, which, h, 1, 2).wait_recv()
+
+    for h in (0, 1):
+        part_arrived(0, h)
+        text_dir[h] += text_in[0, h].astype(F32)
+
+    @pl.when(core == 0)
+    def _():
+        for h in (0, 1):
+            part_arrived(1, h)
+            text_dir[h] += text_in[1, h].astype(F32)
+
+    def text_unit(h):
+        return text_raw[0, h].astype(F32) * text_scale[:, h * hr : (h + 1) * hr]
+
+    for h in (0, 1):
+        tdot_out[:, h * hr : (h + 1) * hr] = jnp.broadcast_to(
+            jnp.sum(text_unit(h) * text_dir[h], axis=0, keepdims=True), (8, hr)
+        )
+    tdot_there = send(tdot_out, tdot_in, other_mp)
+
+    stored = []
+
+    def store(g, of):
+        first, last, _, _, _ = groups[g]
+        for k in range(first, last):
+            block = levels[g][2][0].at[of, (k - first) * half : (k - first + 1) * half]
+            rows_k = pl.ds(pl.multiple_of(of * half, ROW_TILE), half)
+            place = grad_hbm.at[rows_k, k * LANES : (k + 1) * LANES]
+            stored.append(pltpu.make_async_copy(block, place, out_sem.at[len(stored)]))
+            stored[-1].start()
+
     for g, (_, _, order, _, held) in enumerate(groups):
         for k, copy in enumerate(there[g]):
             copy.wait_recv()
             arrived = chunk(g, source_of(order[0], k + 1))
-            relayed.append(send(arrived, arrived, other_core))
-    for copy in relayed:
-        copy.wait_recv()
-    for g, (first, last, _, _, _) in enumerate(groups):
-        result = levels[g][2][0]
-        for c in range(2):
-            for k in range(first, last):
-                rows_k = slice((k - first) * half, (k - first + 1) * half)
-                grad_ref[c * half : (c + 1) * half, k * LANES : (k + 1) * LANES] = result[c, rows_k, :]
+            relayed[g].append(send(arrived, arrived, other_core))
+        store(g, core)
+    tdot_there.wait_recv()
+    tdot = tdot_out[0:1, :] + tdot_in[0:1, :]
+    for h in (0, 1):
+        lanes = slice(h * hr, (h + 1) * hr)
+        cap_out[:, lanes] = (
+            (text_dir[h] - text_unit(h) * tdot[:, lanes]) * text_scale[:, lanes]
+        ).astype(BF16)
+    stored.append(pltpu.make_async_copy(cap_out, cap_hbm, out_sem.at[len(stored)]))
+    stored[-1].start()
+    for g in range(len(groups)):
+        for copy in relayed[g]:
+            copy.wait_recv()
+        store(g, 1 - core)
+    for copy in stored:
+        copy.wait()
 
     for copy in copies.made + [text_copy(0, 1, 0), text_copy(1, 2, 1), relay] + part_copies:
         copy.wait_send()
@@ -476,6 +544,10 @@
     @pl.when(passes_on)
     def _():
         pass_on.wait_send()
+
+    @pl.when(passes_home)
+    def _():
+        pass_home.wait_send()
 
     for s in range(STEPS + 1):
         for h in (0, 1):
@@ -486,7 +558,7 @@
     rows, depth = x_rows.shape
     width = w_half.shape[1]
     half, hr = width // 2, rows // 2
-    vmem, hbm = pl.BlockSpec(memory_space=pltpu.VMEM), pl.BlockSpec(memory_space=pltpu.HBM)
+    hbm = pl.BlockSpec(memory_space=pltpu.HBM)
     smem = pl.BlockSpec(memory_space=pltpu.SMEM)
     buffers = []
     for _, _, _, (n1, n2, n3), (_, r1, r2) in groups_of(width, depth):
@@ -506,8 +578,8 @@
             jax.ShapeDtypeStruct((width, depth), BF16),
             jax.ShapeDtypeStruct((width, rows), BF16),
         ),
-        in_specs=[hbm, hbm, hbm, vmem, smem, smem],
-        out_specs=(smem, vmem, vmem),
+        in_specs=[hbm] * 6,
+        out_specs=(smem, hbm, hbm),
         scratch_shapes=[
             pltpu.VMEM((2, rows, depth), BF16),
             pltpu.VMEM((width, depth), BF16),
@@ -535,11 +607,16 @@
             pltpu.VMEM((8, rows), F32),
             pltpu.VMEM((8, rows), F32),
             *buffers,
+            pltpu.VMEM((width, rows), BF16),
+            pltpu.SemaphoreType.DMA((2 * depth // LANES + 1,)),
             pltpu.VMEM((half, depth), F32),
+            pltpu.VMEM((1, rows), jnp.int32),
+            pltpu.SMEM((1,), F32),
+            pltpu.SMEM((1,), F32),
             pltpu.VMEM((width, hr), BF16),
             pltpu.SemaphoreType.DMA((1,)),
             pltpu.SemaphoreType.DMA((1,)),
-            pltpu.SemaphoreType.DMA((4,)),
+            pltpu.SemaphoreType.DMA((7,)),
             pltpu.SemaphoreType.DMA((5,)),
             pltpu.SemaphoreType.DMA((2, 2)),
             pltpu.SemaphoreType.DMA((3, 2)),

time: 85.3 us -> 81.3 us (0.953)
  Pallas kernels: 78.1 us -> 74 us
    pallas_call x1, Pallas kernels: 78.1 us -> 74 us  [local(): call(x_rows, w_half.T, t_half.T, matched.reshape(1, rows), sharpness, off...]
where the time goes in v4:
time: 81.3 us; the launch traced here: 81 us
  Pallas kernels  74 us (91%)
  between operations  3.76 us (5%)
  local copies, waits for them, and re-layouts  3.25 us (4%)
    pallas_call x1, Pallas kernels, local(): call(x_rows, w_half.T, t_half.T, matched.reshape(1, rows), sharpness, off...  74 us
    unnamed x4, local copies, waits for them, and re-layouts  3.25 us

profile of v4, /device:TPU:1, one launch (start us, length us, event | category | flops | bytes accessed | tf_op | source)
XLA Modules:
  0.0 81.0 jit_solution(6919960062588951705)
XLA Ops:
  1.9 74.0 %shard_map.85 = (f32[1]{0:T(128)}, bf16[576,1152]{1,0:T(8,128)(2,1)}, bf16[576,256]{1,0:T(8,128)(2,1)}) custom-call(bf16[256,1152]{1,0:T(8,128)(2,1)} %x_hbm.1, bf16[576,1152]{1,0:T(8,128)(2,1)} %bitcast.5, bf16[576,256]{1,0:T(8,128)(2,1)} %bitcast.7, s32[1,256]{1,0:T(1,128)} %bitcast.9, f32[1]{0:T(128)S(6)} %copy.12.scale_hbm, f32[1]{0:T(128)S(6)} %copy.13.offset_hbm), custom_call_target="tpu_custom_call" | custom-call | tf_op jit(solution)/shard_map/pallas_call | solution.py:633
  76.7 0.0 copy-start
  76.7 2.5 %copy.15 = bf16[1152,576]{0,1:T(8,128)(2,1)} copy(bf16[1152,576]{0,1:T(8,128)(2,1)} %bitcast.6) | data formatting | bytes 2654208
  79.2 0.0 copy-done
  79.2 0.7 copy.16
Async XLA Ops:
  76.7 2.5 %copy-start = (bf16[576,256]{1,0:T(8,128)(2,1)S(1)}, bf16[576,256]{1,0:T(8,128)(2,1)}, u32[]{:S(2)}) copy-start(bf16[576,256]{1,0:T(8,128)(2,1)} %get-tuple-element.8) | copy-start | bytes 884740

commit v5 on v4

--- a/solution.py
+++ b/solution.py
@@ -97,7 +97,7 @@
     tdot_in,
     *rest,
 ):
-    *buffers, cap_out, out_sem, grad_own, matched_ref, scale_ref, offset_ref, passed, passed_send, passed_recv, load_sem, text_send, text_recv, cos_send, cos_recv, part_send, part_recv, send_sem, recv_sem = rest
+    *buffers, image_dir, cap_out, out_sem, grad_own, matched_ref, scale_ref, offset_ref, passed, passed_send, passed_recv, load_sem, text_send, text_recv, cos_send, cos_recv, part_send, part_recv, send_sem, recv_sem = rest
     width, rows = t_hbm.shape
     depth = x_hbm.shape[1]
     half, hr = width // 2, rows // 2
@@ -323,11 +323,15 @@
         along_unit += jnp.sum(low.astype(F32) * cos, axis=0, keepdims=True)
         direction += dot(text_low[s, h], low, 1, 0)
 
-    image_back = ((direction - image_unit[...] * along_unit) * image_scale).astype(BF16)
-    back[0] = image_back[:half]
-    back[1] = image_back[half:]
-    back_there = send(back.at[1 - core], back_all.at[core], other_core)
-    back_all[core] = back[core]
+    image_dir[...] = direction
+
+    def image_back(of):
+        rows_h = pl.ds(pl.multiple_of(of * half, ROW_TILE), half)
+        return ((image_dir[rows_h, :] - image_unit[rows_h, :] * along_unit) * image_scale).astype(BF16)
+
+    back[...] = image_back(1 - core)
+    back_there = send(back, back_all.at[core], other_core)
+    back_all[core] = image_back(core)
     loss_core[core] = jnp.broadcast_to(loss_rows, (8, rows))
     loss_core_there = send(loss_core.at[core], loss_core.at[core], other_core)
 
@@ -593,7 +597,7 @@
             pltpu.VMEM((3, 2, hr, rows), BF16),
             pltpu.VMEM((3, 2, hr, rows), BF16),
             pltpu.VMEM((3, 2, hr, rows), BF16),
-            pltpu.VMEM((2, half, rows), BF16),
+            pltpu.VMEM((half, rows), BF16),
             pltpu.VMEM((2, half, rows), BF16),
             pltpu.VMEM((2, 8, rows), F32),
             pltpu.VMEM((NX, 8, rows), F32),
@@ -607,6 +611,7 @@
             pltpu.VMEM((8, rows), F32),
             pltpu.VMEM((8, rows), F32),
             *buffers,
+            pltpu.VMEM((width, rows), F32),
             pltpu.VMEM((width, rows), BF16),
             pltpu.SemaphoreType.DMA((2 * depth // LANES + 1,)),
             pltpu.VMEM((half, depth), F32),

time: 81.3 us -> 81.5 us (level)
  no operation moved by 1% of the time
where the time goes in v5:
time: 81.5 us; the launch traced here: 80.6 us
  Pallas kernels  73.6 us (90%)
  between operations  3.76 us (5%)
  local copies, waits for them, and re-layouts  3.25 us (4%)
    pallas_call x1, Pallas kernels, local(): call(x_rows, w_half.T, t_half.T, matched.reshape(1, rows), sharpness, off...  73.6 us
    unnamed x4, local copies, waits for them, and re-layouts  3.25 us

profile of v5, /device:TPU:1, one launch (start us, length us, event | category | flops | bytes accessed | tf_op | source)
XLA Modules:
  0.0 80.6 jit_solution(13621784751891714532)
XLA Ops:
  1.9 73.6 %shard_map.85 = (f32[1]{0:T(128)}, bf16[576,1152]{1,0:T(8,128)(2,1)}, bf16[576,256]{1,0:T(8,128)(2,1)}) custom-call(bf16[256,1152]{1,0:T(8,128)(2,1)} %x_hbm.1, bf16[576,1152]{1,0:T(8,128)(2,1)} %bitcast.5, bf16[576,256]{1,0:T(8,128)(2,1)} %bitcast.7, s32[1,256]{1,0:T(1,128)} %bitcast.9, f32[1]{0:T(128)S(6)} %copy.12.scale_hbm, f32[1]{0:T(128)S(6)} %copy.13.offset_hbm), custom_call_target="tpu_custom_call" | custom-call | tf_op jit(solution)/shard_map/pallas_call | solution.py:638
  76.2 0.0 copy-start
  76.3 2.5 %copy.15 = bf16[1152,576]{0,1:T(8,128)(2,1)} copy(bf16[1152,576]{0,1:T(8,128)(2,1)} %bitcast.6) | data formatting | bytes 2654208
  78.8 0.0 copy-done
  78.8 0.7 copy.16
Async XLA Ops:
  76.2 2.5 %copy-start = (bf16[576,256]{1,0:T(8,128)(2,1)S(1)}, bf16[576,256]{1,0:T(8,128)(2,1)}, u32[]{:S(2)}) copy-start(bf16[576,256]{1,0:T(8,128)(2,1)} %get-tuple-element.8) | copy-start | bytes 884740
